TPU v7x, 768 devices: a whole 4x8x12 slice. The times are simulated.
768 devices in a mesh: blk: 12 (over z_lo, core), col: 64 (over y, x, z_hi).
Axes of the slice: x: 4, y: 8, z: 12 (z_hi: 2, z_lo: 6; z = z_hi * 6 + z_lo), core: 2. Of those that a mesh axis runs over, the one named last changes fastest.
Arguments:
- amplitudes: bfloat16 [2304, 1, 3072], P('blk', None, 'col'), may hold values from -6 to 6
- integrals: bfloat16 [1, 3072, 3072], P(None, 'col', 'blk'), may hold values from -0.109375 to 0.109375
Outputs:
- ladder_residual: float32 [2304, 1, 3072], P('col', None, 'blk')
All inputs are finite; a program needn't handle non-finite values.
Results may differ from a plain program's by a relative error of at most 0.0003.
Values may be sent and summed in bfloat16 or wider, within the bound.
A program may use at most 32 MiB of HBM per device.

v0:
```python
import jax
import jax.numpy as jnp
from jax import lax
from jax.sharding import PartitionSpec as P


def contract(left, right):
    return jnp.einsum("irk,rkb->irb", left, right, preferred_element_type=jnp.float32)


def body(amplitudes, integrals):
    partial_value = contract(lax.all_gather(amplitudes, "blk", axis=0, tiled=True), integrals)
    ladder_sum = lax.psum_scatter(partial_value, "col", scatter_dimension=0, tiled=True)
    return 0.5 * ladder_sum


def solution(mesh):
    return jax.shard_map(
        body,
        mesh=mesh,
        in_specs=(P("blk", None, "col"), P(None, "col", "blk")),
        out_specs=P("col", None, "blk"),
        check_vma=False,
    )
```

profile of v0, /device:TPU:64, one launch (start us, length us, event | category | flops | bytes accessed | tf_op | source)
XLA Modules:
  0.0 1060.4 jit_solution(10201173592837534908)
XLA Ops:
  6.5 0.0 copy-start
  6.5 0.0 all-reduce.3.cloned.1.call-start
  6.5 0.9 copy.6
  7.4 30.3 %all_gather.3 = bf16[2304,1,48]{2,1,0:T(2,128)(2,1)S(1)} all-gather(bf16[192,1,48]{2,1,0:T(2,128)(2,1)S(1)} %copy.6), channel_id=1, replica_groups=mesh['blk'=12,'col'=64] {'blk'}, dimensions={0}, use_global_device_ids=true | all-gather | bytes 239616 | tf_op jit(solution)/shard_map/all_gather | solution.py:12
  37.7 1.4 copy.7
  39.1 0.0 copy-done
  39.1 0.5 convolution_bitcast_fusion
  39.6 4.1 copy.8
  43.7 0.0 all-reduce.3.cloned.1.call-update
  43.7 1.3 dynamic-slice
  45.7 1006.5 %all-reduce.3.cloned.1.call-done = f32[2304,1,256]{2,1,0:T(1,128)} async-done(((f32[2304,1,256]{2,1,0:T(1,128)}), f32[2304,1,256]{2,1,0:T(1,128)}) %all-reduce.3.cloned.1.call-update) | async-done | bytes 2359312
  1052.1 1.4 dynamic-slice_multiply_fusion
Async XLA Ops:
  6.5 32.6 %copy-start = (bf16[1,48,256]{2,1,0:T(8,128)(2,1)S(1)}, bf16[1,48,256]{2,1,0:T(8,128)(2,1)}, u32[]{:S(2)}) copy-start(bf16[1,48,256]{2,1,0:T(8,128)(2,1)} %param.3) | copy-start | bytes 73732
  6.5 1045.6 %all-reduce.3.cloned.1.call-start = ((), (), s32[]{:S(2)}) async-start(), calls=%async_computation | async-start | bytes 4718592
Sparse Core Ops, SparseCore 0:
  43.8 1008.2 all-reduce.2
where the time goes:
time: 1060 us
  waiting for transfers between devices  1010 us (95%)
  blocking collectives  30.3 us (3%)
  between operations  14.1 us (1%)
    unnamed x2, waiting for transfers between devices  1010 us
    all_gather x1, blocking collectives, body(): lax.all_gather(amplitudes, 'blk', axis=0, tiled=True)  30.3 us
  transfers between devices with their start and end apart: 1, of which 1 were waited for; matrix products, arithmetic and copies ran while one was open for 0% of the time, Pallas kernels for 0%

commit v1 on v0

v1 whole, which is shorter than its diff:
```python
import functools

import jax
import jax.numpy as jnp
from jax import lax
from jax.experimental import pallas as pl
from jax.experimental.pallas import tpu as pltpu
from jax.sharding import PartitionSpec as P

MESH = pl.DeviceIdType.MESH
NX, NY, NZ = 4, 8, 6


def device(y, x, zh, zl, core):
    return {"blk": zl * 2 + core, "col": (y * NX + x) * 2 + zh}


def remote(src, dst, send, recv, where):
    return pltpu.make_async_remote_copy(
        src_ref=src, dst_ref=dst, send_sem=send, recv_sem=recv, device_id=where, device_id_type=MESH
    )


def kernel(
    a_ref, b_ref, out_ref,
    a_own, a_line, a_whole, a_half, b_all, part, near, far, total,
    local_sem, line_send, line_recv, row_send, row_recv, pair_send, pair_recv,
    b_send, b_recv, near_send, near_recv, far_send, far_recv,
):
    blk, col = lax.axis_index("blk"), lax.axis_index("col")
    zl, core = blk // 2, blk % 2
    zh, x, y = col % 2, (col // 2) % NX, col // (2 * NX)
    at = functools.partial(device)

    load_a = pltpu.make_async_copy(a_ref, a_own, local_sem.at[0])
    load_b = pltpu.make_async_copy(b_ref, b_all.at[0], local_sem.at[1])
    load_a.start()
    load_b.start()

    barrier = pltpu.get_barrier_semaphore()

    def greet(where):
        pl.semaphore_signal(barrier, inc=1, device_id=where, device_id_type=MESH)

    greet(at(y, x, 1 - zh, zl, core))
    for d in range(1, NY):
        greet(at((y + d) % NY, x, zh, zl, core))
    for d in range(1, NZ):
        greet(at(y, x, zh, (zl + d) % NZ, core))
    for d in range(1, NX):
        greet(at(y, (x + d) % NX, zh, zl, core))
    greet(at(y, x, zh, zl, 1 - core))

    load_a.wait()
    mine = a_own[...]
    a_line[zl, 0] = mine[:, 0:128]
    a_line[zl, 1] = jnp.concatenate([mine[:, 96:192], mine[:, 64:96]], axis=1)
    pl.semaphore_wait(barrier, NY + NZ + NX - 1)

    line = [
        remote(a_line.at[zl], a_line.at[zl], line_send.at[d], line_recv.at[d], at(y, x, zh, (zl + d) % NZ, core))
        for d in range(1, NZ)
    ]
    for copy in line:
        copy.start()
    ring = [
        remote(b_ref, b_all.at[d], b_send.at[d], b_recv.at[d], at((y + d) % NY, x, zh, zl, core))
        for d in range(1, NY)
    ]
    for copy in ring:
        copy.start()

    for copy in line:
        copy.wait_recv()

    def rows(d):
        to = (y + d) % NY
        pair, odd = to // 2, to % 2
        whole = remote(
            a_line.at[(3 * pair + 2 * odd) // 2], a_whole.at[d], row_send.at[d], row_recv.at[d], at(to, x, zh, zl, core)
        )
        half = remote(
            a_line.at[(3 * pair + 1) // 2, odd], a_half.at[d], row_send.at[d], row_recv.at[d], at(to, x, zh, zl, core)
        )
        return core == pair % 2, whole, half

    for d in range(1, NY):
        is_whole, whole, half = rows(d)

        @pl.when(is_whole)
        def _():
            whole.start()

        @pl.when(jnp.logical_not(is_whole))
        def _():
            half.start()

    odd = y % 2
    have_whole = core == (y // 2) % 2
    sibling = at(y, x, zh, zl, 1 - core)
    own_whole = a_line.at[(3 * (y // 2) + 2 * odd) // 2]
    own_half = a_line.at[(3 * (y // 2) + 1) // 2, odd]

    def give(buffer, own, d):
        return remote(own if d == 0 else buffer.at[d], buffer.at[d], pair_send.at[d], pair_recv.at[d], sibling)

    @pl.when(have_whole)
    def _():
        give(a_whole, own_whole, 0).start()
        a_whole[0] = own_whole[...]
        for d in range(1, NY):
            remote(own_whole, a_whole.at[d], row_send.at[d], row_recv.at[d], sibling).wait_recv()
            give(a_whole, own_whole, d).start()
        for d in range(NY):
            give(a_half, own_half, d).wait_recv()

    @pl.when(jnp.logical_not(have_whole))
    def _():
        give(a_half, own_half, 0).start()
        a_half[0] = own_half[...]
        for d in range(1, NY):
            remote(own_half, a_half.at[d], row_send.at[d], row_recv.at[d], sibling).wait_recv()
            give(a_half, own_half, d).start()
        for d in range(NY):
            give(a_whole, own_whole, d).wait_recv()

    load_b.wait()
    for copy in ring:
        copy.wait_recv()

    depth = NY * 48
    right = b_all[...].reshape(depth, 256)
    w0 = a_whole[:, 0].reshape(depth, 128)
    w1 = a_whole[:, 1].reshape(depth, 128)
    h = a_half[...].reshape(depth, 128)
    units = [jnp.where(odd == 1, h, w0), jnp.where(odd == 1, w0, w1), jnp.where(odd == 1, w1, h)]
    for j, unit in enumerate(units):
        value = lax.dot_general(unit, right, (((0,), (0,)), ((), ())), preferred_element_type=jnp.float32)
        row = 96 * j
        while row < 96 * (j + 1):
            block, offset = row // 36, row % 36
            count = min(36 - offset, 96 * (j + 1) - row)
            piece = value[row - 96 * j : row - 96 * j + count]
            part[block, offset : offset + count] = piece[:, 0:128]
            part[block, 36 + offset : 36 + offset + count] = piece[:, 128:256]
            row += count

    def to_near(kind, d):
        half_of = (1 - zh) if kind == 0 else zh
        to = (x + d) % NX
        return remote(
            part.at[to * 2 + half_of], near.at[kind, d], near_send.at[kind, d], near_recv.at[kind, d],
            at(y, to, zh, zl, core),
        )

    for kind in range(2):
        for d in range(1, NX):
            to_near(kind, d).start()
    for d in range(1, NX):
        to_near(0, d).wait_recv()
    total[0] = part[x * 2 + 1 - zh] + near[0, 1] + (near[0, 2] + near[0, 3])
    over = remote(total.at[0], far, far_send, far_recv, at(y, x, 1 - zh, zl, core))
    over.start()
    for d in range(1, NX):
        to_near(1, d).wait_recv()
    total[1] = part[x * 2 + zh] + near[1, 1] + (near[1, 2] + near[1, 3])
    over.wait_recv()
    result = 0.5 * (total[1] + far[...])
    out_ref[pl.ds(0, 36, stride=2), :] = result[0:36]
    out_ref[pl.ds(1, 36, stride=2), :] = result[36:72]

    over.wait_send()
    for kind in range(2):
        for d in range(1, NX):
            to_near(kind, d).wait_send()
    for copy in line + ring:
        copy.wait_send()
    for d in range(1, NY):
        is_whole, whole, half = rows(d)

        @pl.when(is_whole)
        def _():
            whole.wait_send()

        @pl.when(jnp.logical_not(is_whole))
        def _():
            half.wait_send()

    @pl.when(have_whole)
    def _():
        for d in range(NY):
            give(a_whole, own_whole, d).wait_send()

    @pl.when(jnp.logical_not(have_whole))
    def _():
        for d in range(NY):
            give(a_half, own_half, d).wait_send()


def body(amplitudes, integrals):
    left = jnp.transpose(amplitudes, (1, 2, 0)).reshape(48, 192)
    right = integrals.reshape(48, 256)
    dma = pltpu.SemaphoreType.DMA
    out = pl.pallas_call(
        kernel,
        out_shape=jax.ShapeDtypeStruct((72, 128), jnp.float32),
        in_specs=[pl.BlockSpec(memory_space=pl.ANY)] * 2,
        out_specs=pl.BlockSpec(memory_space=pltpu.VMEM),
        scratch_shapes=[
            pltpu.VMEM((48, 192), jnp.bfloat16),
            pltpu.VMEM((NZ, 2, 48, 128), jnp.bfloat16),
            pltpu.VMEM((NY, 2, 48, 128), jnp.bfloat16),
            pltpu.VMEM((NY, 48, 128), jnp.bfloat16),
            pltpu.VMEM((NY, 48, 256), jnp.bfloat16),
            pltpu.VMEM((8, 72, 128), jnp.float32),
            pltpu.VMEM((2, NX, 72, 128), jnp.float32),
            pltpu.VMEM((72, 128), jnp.float32),
            pltpu.VMEM((2, 72, 128), jnp.float32),
            dma((2,)), dma((NZ,)), dma((NZ,)), dma((NY,)), dma((NY,)), dma((NY,)), dma((NY,)),
            dma((NY,)), dma((NY,)), dma((2, NX)), dma((2, NX)), dma, dma,
        ],
        compiler_params=pltpu.CompilerParams(collective_id=0, has_side_effects=True),
    )(left, right)
    return out.reshape(36, 1, 256)


def solution(mesh):
    return jax.shard_map(
        body,
        mesh=mesh,
        in_specs=(P("blk", None, "col"), P(None, "col", "blk")),
        out_specs=P("col", None, "blk"),
        check_vma=False,
    )
```

time: 1060 us -> 45.2 us (0.04)
  the two profiles are of different devices: /device:TPU:64 before, /device:TPU:1 now
where the time goes in v1:
time: 45.2 us; the launch traced here: 45 us
  Pallas kernels  43.6 us (96%)
  local copies, waits for them, and re-layouts  1.39 us (3%)
    pallas_call x1, Pallas kernels, body(): pl.pallas_call(kernel, out_shape=jax.ShapeDtypeStruct((72, 128), jnp.floa...  43.6 us
    unnamed x1, local copies, waits for them, and re-layouts  1.39 us

profile of v1, /device:TPU:1, one launch (start us, length us, event | category | flops | bytes accessed | tf_op | source)
XLA Modules:
  0.0 45.0 jit_solution(4291975506115182856)
XLA Ops:
  0.0 43.6 %shard_map.28 = f32[72,128]{1,0:T(8,128)} custom-call(bf16[48,192]{1,0:T(8,128)(2,1)} %bitcast.6, bf16[48,256]{1,0:T(8,128)(2,1)} %bitcast.7), custom_call_target="tpu_custom_call" | custom-call | tf_op jit(solution)/shard_map/pallas_call | solution.py:204
  43.6 1.4 %copy.6 = f32[36,1,256]{2,1,0:T(1,128)} copy(f32[36,1,256]{2,1,0:T(1,128)} %bitcast.5) | data formatting | bytes 73728

commit v2 on v0

v2 whole, which is shorter than its diff:
```python
import jax
import jax.numpy as jnp
from jax import lax
from jax.experimental import pallas as pl
from jax.experimental.pallas import tpu as pltpu
from jax.sharding import PartitionSpec as P

MESH = pl.DeviceIdType.MESH
NX, NY, NL, NZ = 4, 8, 6, 12
RING_Y = (4, 3, 5, 2, 6, 1, 7)


def device(y, x, z, core):
    return {"blk": (z % NL) * 2 + core, "col": (y * NX + x) * 2 + z // NL}


def remote(src, dst, send, recv, where):
    return pltpu.make_async_remote_copy(
        src_ref=src, dst_ref=dst, send_sem=send, recv_sem=recv, device_id=where, device_id_type=MESH
    )


def chosen(block, wide, to, half):
    lane = lax.broadcasted_iota(jnp.int32, (192, 128), 1)
    row = lax.broadcasted_iota(jnp.int32, (192, 128), 0)
    slot = (lane >= 40).astype(jnp.int32) + (lane >= 80).astype(jnp.int32) + (lane >= 120).astype(jnp.int32)
    inner = lane - 40 * slot
    odd = to % 2
    first = jnp.where(wide, odd, 2 - 2 * odd)
    slots = jnp.where(wide, 3, 2)
    source = 288 * to - 192 * block + 36 * half + 72 * (slot + first) + inner
    hit = (source == row) & (inner < 36) & (slot < slots)
    return jnp.where(hit, 1.0, 0.0).astype(jnp.bfloat16)


def kernel(
    a_ref, b_ref, out_ref,
    a_own, tiles, a_all, b_all, part, near,
    local_sem, tile_send, tile_recv, pair_send, pair_recv,
    own_send, own_recv, far_send, far_recv, near_send, near_recv, answer, answer_far,
):
    blk, col = lax.axis_index("blk"), lax.axis_index("col")
    zl, core = blk // 2, blk % 2
    zh, x, y = col % 2, (col // 2) % NX, col // (2 * NX)
    z = zh * NL + zl
    slot, other = zh * NY + y, (1 - zh) * NY + y

    load_a = pltpu.make_async_copy(a_ref, a_own, local_sem.at[0])
    load_b = pltpu.make_async_copy(b_ref, b_all.at[slot], local_sem.at[1])
    load_a.start()
    load_b.start()

    split = blk % 3 == 1
    targets = (2 * (blk // 3) + (blk % 3) // 2, 2 * (blk // 3) + 1)
    pair = y // 2
    kind = jnp.where(core == pair % 2, 0, 1)
    giver = jnp.where(kind == 0, (3 * pair + 2 * (y % 2)) // 2, (3 * pair + 1) // 2)
    gives_self = zl == giver
    sent_kind = jnp.where(split, 1, 0)
    sibling = device(y, x, z, 1 - core)

    barrier = pltpu.get_barrier_semaphore()

    def greet(where):
        pl.semaphore_signal(barrier, inc=1, device_id=where, device_id_type=MESH)

    def providers():
        for half in (0, 1):
            at = half * NL + giver
            for d in range(NY):
                yield at, device((y + d) % NY, x, at, core)

    def signal(sem, where):
        pl.semaphore_signal(sem, inc=1, device_id=where, device_id_type=MESH)

    for d in RING_Y:
        greet(device((y + d) % NY, x, z, core))
    for d in range(1, NX):
        greet(device(y, (x + d) % NX, z, core))
    greet(sibling)
    for at, where in providers():

        @pl.when(at > z)
        def _():
            greet(where)

    for to in range(1, NZ):

        @pl.when(to > z)
        def _():
            greet(device(targets[0], x, to, core))

        @pl.when((to > z) & split)
        def _():
            greet(device(targets[1], x, to, core))

    @pl.when(z < NL)
    def _():
        greet(device(y, x, z + NL, core))

    load_a.wait()
    mine = a_own[...]

    def make(k, half):
        wide = jnp.logical_not(split)
        tile = jnp.dot(mine, chosen(blk, wide, targets[k], half), preferred_element_type=jnp.float32)
        tiles[k, half] = tile.astype(jnp.bfloat16)

    make(0, 0)
    make(0, 1)

    @pl.when(split)
    def _():
        make(1, 0)
        make(1, 1)

    per_plane = jnp.where(split, 2, 1)
    lower = jnp.where(giver < z, 1, 0) + jnp.where(NL + giver < z, 1, 0)
    partners = (NY - 1) + (NX - 1) + 1 + per_plane * z + NY * lower + jnp.where(z >= NL, 1, 0)
    pl.semaphore_wait(barrier, partners)

    across = remote(b_ref, b_all.at[slot], far_send.at[0], far_recv.at[0], device(y, x, (z + NL) % NZ, core))

    @pl.when(z >= NL)
    def _():
        signal(answer_far, device(y, x, z - NL, core))
        across.start()

    for at, where in providers():

        @pl.when(at < z)
        def _():
            signal(answer.at[z], where)

    def tile_copy(k, to):
        return remote(
            tiles.at[k, to // NL], a_all.at[sent_kind, slot], tile_send.at[k, to], tile_recv.at[slot],
            device(targets[k], x, to, core),
        )

    def each_tile(to, act):
        @pl.when((to != z) | (targets[0] != y))
        def _():
            act(tile_copy(0, to))

        @pl.when(split & ((to != z) | (targets[1] != y)))
        def _():
            act(tile_copy(1, to))

    def start_tiles(planes, low):
        for to in planes:

            @pl.when(to <= z if low else to > z)
            def _():
                if not low:
                    pl.semaphore_wait(answer.at[to], per_plane)
                each_tile(to, lambda copy: copy.start())

    start_tiles(range(NZ), True)

    own = [
        remote(b_ref, b_all.at[slot], own_send.at[d], own_recv.at[d], device((y + d) % NY, x, z, core))
        for d in RING_Y
    ]
    for copy in own:
        copy.start()
    start_tiles(range(1, NL), False)

    @pl.when(z < NL)
    def _():
        pl.semaphore_wait(answer_far, 1)
        across.start()

    @pl.when(gives_self)
    def _():
        a_all[kind, slot] = tiles[jnp.where(split & (targets[1] == y), 1, 0), zh]

    across.wait_recv()
    rest = [
        remote(b_all.at[other], b_all.at[other], far_send.at[d], far_recv.at[d], device((y + d) % NY, x, z, core))
        for d in RING_Y
    ]
    for copy in rest:
        copy.start()

    start_tiles(range(NL, NZ), False)

    def arrival(s):
        return remote(a_all.at[kind, s], a_all.at[kind, s], tile_send.at[0, 0], tile_recv.at[s], sibling)

    def give(s):
        return remote(a_all.at[kind, s], a_all.at[kind, s], pair_send.at[s], pair_recv.at[s], sibling)

    def take(s):
        return remote(a_all.at[1 - kind, s], a_all.at[1 - kind, s], pair_send.at[s], pair_recv.at[s], sibling)

    @pl.when(jnp.logical_not(gives_self))
    def _():
        arrival(slot).wait_recv()

    give(slot).start()
    for d in range(1, NY):
        s = zh * NY + (y + d) % NY
        arrival(s).wait_recv()
        give(s).start()
    for d in range(NY):
        s = (1 - zh) * NY + (y + d) % NY
        arrival(s).wait_recv()
        give(s).start()
    for s in range(2 * NY):
        take(s).wait_recv()

    load_b.wait()
    for copy in own:
        copy.wait_recv()

    depth = NY * 48

    def product(k, base):
        left = a_all[k, pl.ds(base, NY)].reshape(depth, 128)
        right = b_all[pl.ds(base, NY)].reshape(depth, 256)
        return lax.dot_general(left, right, (((0,), (0,)), ((), ())), preferred_element_type=jnp.float32)

    base, far_base = zh * NY, (1 - zh) * NY
    wide, narrow = product(0, base), product(1, base)
    for copy in rest:
        copy.wait_recv()
    wide += product(0, far_base)
    narrow += product(1, far_base)
    w = [wide[40 * i : 40 * i + 36] for i in range(3)]
    n = [narrow[40 * i : 40 * i + 36] for i in range(2)]
    odd = y % 2 == 1
    sums = (
        jnp.where(odd, n[0], w[0]),
        jnp.where(odd, n[1] + w[0], w[1]),
        jnp.where(odd, w[1], w[2] + n[0]),
        jnp.where(odd, w[2], n[1]),
    )
    for i, value in enumerate(sums):
        part[i, 0:36] = value[:, 0:128]
        part[i, 36:72] = value[:, 128:256]

    gather = []
    for d in (2, 1, 3):
        to = (x + d) % NX
        gather.append(remote(part.at[to], near.at[d], near_send.at[d], near_recv.at[d], device(y, to, z, core)))
    for copy in gather:
        copy.start()
    for copy in gather:
        copy.wait_recv()
    result = 0.5 * ((part[x] + near[1]) + (near[2] + near[3]))
    out_ref[pl.ds(0, 36, stride=2), :] = result[0:36]
    out_ref[pl.ds(1, 36, stride=2), :] = result[36:72]

    across.wait_send()
    for to in range(NZ):
        each_tile(to, lambda copy: copy.wait_send())
    for s in range(2 * NY):
        give(s).wait_send()
    for copy in own + rest + gather:
        copy.wait_send()


def body(amplitudes, integrals):
    left = jnp.transpose(amplitudes, (1, 2, 0)).reshape(48, 192)
    right = integrals.reshape(48, 256)
    dma = pltpu.SemaphoreType.DMA
    out = pl.pallas_call(
        kernel,
        out_shape=jax.ShapeDtypeStruct((72, 128), jnp.float32),
        in_specs=[pl.BlockSpec(memory_space=pl.ANY)] * 2,
        out_specs=pl.BlockSpec(memory_space=pltpu.VMEM),
        scratch_shapes=[
            pltpu.VMEM((48, 192), jnp.bfloat16),
            pltpu.VMEM((2, 2, 48, 128), jnp.bfloat16),
            pltpu.VMEM((2, 2 * NY, 48, 128), jnp.bfloat16),
            pltpu.VMEM((2 * NY, 48, 256), jnp.bfloat16),
            pltpu.VMEM((NX, 72, 128), jnp.float32),
            pltpu.VMEM((NX, 72, 128), jnp.float32),
            dma((2,)), dma((2, NZ)), dma((2 * NY,)), dma((2 * NY,)), dma((2 * NY,)),
            dma((NY,)), dma((NY,)), dma((NY,)), dma((NY,)), dma((NX,)), dma((NX,)),
            pltpu.SemaphoreType.REGULAR((NZ,)), pltpu.SemaphoreType.REGULAR,
        ],
        compiler_params=pltpu.CompilerParams(collective_id=0, has_side_effects=True),
    )(left, right)
    return out.reshape(36, 1, 256)


def solution(mesh):
    return jax.shard_map(
        body,
        mesh=mesh,
        in_specs=(P("blk", None, "col"), P(None, "col", "blk")),
        out_specs=P("col", None, "blk"),
        check_vma=False,
    )
```

time: 1060 us -> 37.3 us (0.04)
  the two profiles are of different devices: /device:TPU:64 before, /device:TPU:256 now
where the time goes in v2:
time: 37.3 us; the launch traced here: 37 us
  Pallas kernels  35.6 us (95%)
  local copies, waits for them, and re-layouts  1.39 us (4%)
    pallas_call x1, Pallas kernels, body(): pl.pallas_call(kernel, out_shape=jax.ShapeDtypeStruct((72, 128), jnp.floa...  35.6 us
    unnamed x1, local copies, waits for them, and re-layouts  1.39 us

profile of v2, /device:TPU:256, one launch (start us, length us, event | category | flops | bytes accessed | tf_op | source)
XLA Modules:
  0.0 37.0 jit_solution(215431691828510121)
XLA Ops:
  0.0 35.6 %shard_map.28 = f32[72,128]{1,0:T(8,128)} custom-call(bf16[48,192]{1,0:T(8,128)(2,1)} %bitcast.6, bf16[48,256]{1,0:T(8,128)(2,1)} %bitcast.7), custom_call_target="tpu_custom_call" | custom-call | tf_op jit(solution)/shard_map/pallas_call | solution.py:268
  35.6 1.4 %copy.6 = f32[36,1,256]{2,1,0:T(1,128)} copy(f32[36,1,256]{2,1,0:T(1,128)} %bitcast.5) | data formatting | bytes 73728

commit v3 on v2

--- a/solution.py
+++ b/solution.py
@@ -37,7 +37,7 @@
     a_ref, b_ref, out_ref,
     a_own, tiles, a_all, b_all, part, near,
     local_sem, tile_send, tile_recv, pair_send, pair_recv,
-    own_send, own_recv, far_send, far_recv, near_send, near_recv, answer, answer_far,
+    own_send, own_recv, far_send, far_recv, near_send, near_recv, answer, answer_far, answer_y, answer_x,
 ):
     blk, col = lax.axis_index("blk"), lax.axis_index("col")
     zl, core = blk // 2, blk % 2
@@ -73,10 +73,21 @@
     def signal(sem, where):
         pl.semaphore_signal(sem, inc=1, device_id=where, device_id_type=MESH)
 
+    def rank(at):
+        return jnp.where(at < 4, at, 11 - at)
+
+    for d in range(1, NX):
+
+        @pl.when((x + d) % NX > x)
+        def _():
+            greet(device(y, (x + d) % NX, z, core))
+
     for d in RING_Y:
-        greet(device((y + d) % NY, x, z, core))
-    for d in range(1, NX):
-        greet(device(y, (x + d) % NX, z, core))
+
+        @pl.when(rank((y + d) % NY) > rank(y))
+        def _():
+            greet(device((y + d) % NY, x, z, core))
+
     greet(sibling)
     for at, where in providers():
 
@@ -97,6 +108,36 @@
     @pl.when(z < NL)
     def _():
         greet(device(y, x, z + NL, core))
+
+    per_plane = jnp.where(split, 2, 1)
+    lower = jnp.where(giver < z, 1, 0) + jnp.where(NL + giver < z, 1, 0)
+    partners = rank(y) + x + 1 + per_plane * z + NY * lower + jnp.where(z >= NL, 1, 0)
+    pl.semaphore_wait(barrier, partners)
+
+    across = remote(b_ref, b_all.at[slot], far_send.at[0], far_recv.at[0], device(y, x, (z + NL) % NZ, core))
+
+    @pl.when(z >= NL)
+    def _():
+        signal(answer_far, device(y, x, z - NL, core))
+        across.start()
+
+    for at, where in providers():
+
+        @pl.when(at < z)
+        def _():
+            signal(answer.at[z], where)
+
+    for d in range(1, NY):
+
+        @pl.when(rank((y + d) % NY) < rank(y))
+        def _():
+            signal(answer_y.at[NY - d], device((y + d) % NY, x, z, core))
+
+    for d in range(1, NX):
+
+        @pl.when((x + d) % NX < x)
+        def _():
+            signal(answer_x.at[NX - d], device(y, (x + d) % NX, z, core))
 
     load_a.wait()
     mine = a_own[...]
@@ -113,24 +154,6 @@
     def _():
         make(1, 0)
         make(1, 1)
-
-    per_plane = jnp.where(split, 2, 1)
-    lower = jnp.where(giver < z, 1, 0) + jnp.where(NL + giver < z, 1, 0)
-    partners = (NY - 1) + (NX - 1) + 1 + per_plane * z + NY * lower + jnp.where(z >= NL, 1, 0)
-    pl.semaphore_wait(barrier, partners)
-
-    across = remote(b_ref, b_all.at[slot], far_send.at[0], far_recv.at[0], device(y, x, (z + NL) % NZ, core))
-
-    @pl.when(z >= NL)
-    def _():
-        signal(answer_far, device(y, x, z - NL, core))
-        across.start()
-
-    for at, where in providers():
-
-        @pl.when(at < z)
-        def _():
-            signal(answer.at[z], where)
 
     def tile_copy(k, to):
         return remote(
@@ -150,13 +173,18 @@
     def start_tiles(planes, low):
         for to in planes:
 
-            @pl.when(to <= z if low else to > z)
+            @pl.when(to < z if low else to > z)
             def _():
                 if not low:
                     pl.semaphore_wait(answer.at[to], per_plane)
                 each_tile(to, lambda copy: copy.start())
 
-    start_tiles(range(NZ), True)
+    start_tiles(range(NZ - 1), True)
+    for d in RING_Y:
+
+        @pl.when(rank((y + d) % NY) > rank(y))
+        def _():
+            pl.semaphore_wait(answer_y.at[d], 1)
 
     own = [
         remote(b_ref, b_all.at[slot], own_send.at[d], own_recv.at[d], device((y + d) % NY, x, z, core))
@@ -164,6 +192,7 @@
     ]
     for copy in own:
         copy.start()
+    each_tile(z, lambda copy: copy.start())
     start_tiles(range(1, NL), False)
 
     @pl.when(z < NL)
@@ -240,6 +269,12 @@
         part[i, 0:36] = value[:, 0:128]
         part[i, 36:72] = value[:, 128:256]
 
+    for d in range(1, NX):
+
+        @pl.when((x + d) % NX > x)
+        def _():
+            pl.semaphore_wait(answer_x.at[d], 1)
+
     gather = []
     for d in (2, 1, 3):
         to = (x + d) % NX
@@ -267,7 +302,7 @@
     dma = pltpu.SemaphoreType.DMA
     out = pl.pallas_call(
         kernel,
-        out_shape=jax.ShapeDtypeStruct((72, 128), jnp.float32),
+        out_shape=pltpu.VMEM((72, 128), jnp.float32),
         in_specs=[pl.BlockSpec(memory_space=pl.ANY)] * 2,
         out_specs=pl.BlockSpec(memory_space=pltpu.VMEM),
         scratch_shapes=[
@@ -280,6 +315,7 @@
             dma((2,)), dma((2, NZ)), dma((2 * NY,)), dma((2 * NY,)), dma((2 * NY,)),
             dma((NY,)), dma((NY,)), dma((NY,)), dma((NY,)), dma((NX,)), dma((NX,)),
             pltpu.SemaphoreType.REGULAR((NZ,)), pltpu.SemaphoreType.REGULAR,
+            pltpu.SemaphoreType.REGULAR((NY,)), pltpu.SemaphoreType.REGULAR((NX,)),
         ],
         compiler_params=pltpu.CompilerParams(collective_id=0, has_side_effects=True),
     )(left, right)

time: 37.3 us -> 35.6 us (0.954)
  the two profiles are of different devices: /device:TPU:256 before, /device:TPU:192 now
where the time goes in v3:
time: 35.6 us; the launch traced here: 35.4 us
  Pallas kernels  34.8 us (98%)
  local copies, waits for them, and re-layouts  0.62 us (2%)
    pallas_call x1, Pallas kernels, body(): pl.pallas_call(kernel, out_shape=pltpu.VMEM((72, 128), jnp.float32), in_s...  34.8 us

profile of v3, /device:TPU:192, one launch (start us, length us, event | category | flops | bytes accessed | tf_op | source)
XLA Modules:
  0.0 35.4 jit_solution(6106778425125187446)
XLA Ops:
  0.0 34.8 %shard_map.28 = f32[72,128]{1,0:T(8,128)S(1)} custom-call(bf16[48,192]{1,0:T(8,128)(2,1)} %bitcast.6, bf16[48,256]{1,0:T(8,128)(2,1)} %bitcast.7), custom_call_target="tpu_custom_call" | custom-call | tf_op jit(solution)/shard_map/pallas_call | solution.py:303
  34.8 0.6 %copy.6 = f32[36,1,256]{2,1,0:T(1,128)} copy(f32[36,1,256]{2,1,0:T(1,128)S(1)} %bitcast.5) | data formatting | bytes 73728

commit v4 on v3

--- a/solution.py
+++ b/solution.py
@@ -8,6 +8,7 @@
 MESH = pl.DeviceIdType.MESH
 NX, NY, NL, NZ = 4, 8, 6, 12
 RING_Y = (4, 3, 5, 2, 6, 1, 7)
+ORDER_Y = (0, 1, 2, 3, 7, 6, 5, 4)
 
 
 def device(y, x, z, core):
@@ -37,7 +38,7 @@
     a_ref, b_ref, out_ref,
     a_own, tiles, a_all, b_all, part, near,
     local_sem, tile_send, tile_recv, pair_send, pair_recv,
-    own_send, own_recv, far_send, far_recv, near_send, near_recv, answer, answer_far, answer_y, answer_x,
+    own_send, own_recv, rest_send, rest_recv, far_send, far_recv, near_send, near_recv, answer, answer_far, answer_y, answer_x,
 ):
     blk, col = lax.axis_index("blk"), lax.axis_index("col")
     zl, core = blk // 2, blk % 2
@@ -186,12 +187,26 @@
         def _():
             pl.semaphore_wait(answer_y.at[d], 1)
 
-    own = [
-        remote(b_ref, b_all.at[slot], own_send.at[d], own_recv.at[d], device((y + d) % NY, x, z, core))
-        for d in RING_Y
-    ]
-    for copy in own:
-        copy.start()
+    def round_y(src, into, send, recv, act):
+        for to in ORDER_Y:
+
+            @pl.when(to != y)
+            def _():
+                act(remote(src, b_all.at[into], send.at[to], recv.at[y], device(to, x, z, core)))
+
+    def own_copies(act):
+        round_y(b_ref, slot, own_send, own_recv, act)
+
+    def rest_copies(act):
+        round_y(b_all.at[other], other, rest_send, rest_recv, act)
+
+    def from_y(half, recv):
+        for d in range(1, NY):
+            at = (y + d) % NY
+            block = b_all.at[half * NY + at]
+            remote(block, block, own_send.at[0], recv.at[at], sibling).wait_recv()
+
+    own_copies(lambda copy: copy.start())
     each_tile(z, lambda copy: copy.start())
     start_tiles(range(1, NL), False)
 
@@ -205,12 +220,7 @@
         a_all[kind, slot] = tiles[jnp.where(split & (targets[1] == y), 1, 0), zh]
 
     across.wait_recv()
-    rest = [
-        remote(b_all.at[other], b_all.at[other], far_send.at[d], far_recv.at[d], device((y + d) % NY, x, z, core))
-        for d in RING_Y
-    ]
-    for copy in rest:
-        copy.start()
+    rest_copies(lambda copy: copy.start())
 
     start_tiles(range(NL, NZ), False)
 
@@ -240,8 +250,7 @@
         take(s).wait_recv()
 
     load_b.wait()
-    for copy in own:
-        copy.wait_recv()
+    from_y(zh, own_recv)
 
     depth = NY * 48
 
@@ -252,8 +261,7 @@
 
     base, far_base = zh * NY, (1 - zh) * NY
     wide, narrow = product(0, base), product(1, base)
-    for copy in rest:
-        copy.wait_recv()
+    from_y(1 - zh, rest_recv)
     wide += product(0, far_base)
     narrow += product(1, far_base)
     w = [wide[40 * i : 40 * i + 36] for i in range(3)]
@@ -275,14 +283,17 @@
         def _():
             pl.semaphore_wait(answer_x.at[d], 1)
 
-    gather = []
-    for d in (2, 1, 3):
-        to = (x + d) % NX
-        gather.append(remote(part.at[to], near.at[d], near_send.at[d], near_recv.at[d], device(y, to, z, core)))
-    for copy in gather:
-        copy.start()
-    for copy in gather:
-        copy.wait_recv()
+    def sums_x(act):
+        for to in range(NX):
+            d = jnp.where(to > x, to - x, to - x + NX)
+
+            @pl.when(to != x)
+            def _():
+                act(remote(part.at[to], near.at[d], near_send.at[d], near_recv.at[d], device(y, to, z, core)))
+
+    sums_x(lambda copy: copy.start())
+    for d in range(1, NX):
+        remote(near.at[d], near.at[d], near_send.at[d], near_recv.at[d], sibling).wait_recv()
     result = 0.5 * ((part[x] + near[1]) + (near[2] + near[3]))
     out_ref[pl.ds(0, 36, stride=2), :] = result[0:36]
     out_ref[pl.ds(1, 36, stride=2), :] = result[36:72]
@@ -292,8 +303,9 @@
         each_tile(to, lambda copy: copy.wait_send())
     for s in range(2 * NY):
         give(s).wait_send()
-    for copy in own + rest + gather:
-        copy.wait_send()
+    own_copies(lambda copy: copy.wait_send())
+    rest_copies(lambda copy: copy.wait_send())
+    sums_x(lambda copy: copy.wait_send())
 
 
 def body(amplitudes, integrals):
@@ -313,7 +325,7 @@
             pltpu.VMEM((NX, 72, 128), jnp.float32),
             pltpu.VMEM((NX, 72, 128), jnp.float32),
             dma((2,)), dma((2, NZ)), dma((2 * NY,)), dma((2 * NY,)), dma((2 * NY,)),
-            dma((NY,)), dma((NY,)), dma((NY,)), dma((NY,)), dma((NX,)), dma((NX,)),
+            dma((NY,)), dma((NY,)), dma((NY,)), dma((NY,)), dma((1,)), dma((1,)), dma((NX,)), dma((NX,)),
             pltpu.SemaphoreType.REGULAR((NZ,)), pltpu.SemaphoreType.REGULAR,
             pltpu.SemaphoreType.REGULAR((NY,)), pltpu.SemaphoreType.REGULAR((NX,)),
         ],

time: 35.6 us -> 35.1 us (0.986)
  the two profiles are of different devices: /device:TPU:192 before, /device:TPU:224 now
where the time goes in v4:
time: 35.1 us; the launch traced here: 34.9 us
  Pallas kernels  34.3 us (98%)
  local copies, waits for them, and re-layouts  0.62 us (2%)
    pallas_call x1, Pallas kernels, body(): pl.pallas_call(kernel, out_shape=pltpu.VMEM((72, 128), jnp.float32), in_s...  34.3 us

profile of v4, /device:TPU:224, one launch (start us, length us, event | category | flops | bytes accessed | tf_op | source)
XLA Modules:
  0.0 34.9 jit_solution(5325958150140515481)
XLA Ops:
  0.0 34.3 %shard_map.28 = f32[72,128]{1,0:T(8,128)S(1)} custom-call(bf16[48,192]{1,0:T(8,128)(2,1)} %bitcast.6, bf16[48,256]{1,0:T(8,128)(2,1)} %bitcast.7), custom_call_target="tpu_custom_call" | custom-call | tf_op jit(solution)/shard_map/pallas_call | solution.py:315
  34.3 0.6 %copy.6 = f32[36,1,256]{2,1,0:T(1,128)} copy(f32[36,1,256]{2,1,0:T(1,128)S(1)} %bitcast.5) | data formatting | bytes 73728

commit v5 on v4

--- a/solution.py
+++ b/solution.py
@@ -7,6 +7,7 @@
 
 MESH = pl.DeviceIdType.MESH
 NX, NY, NL, NZ = 4, 8, 6, 12
+DEPTH = (48, 32)
 RING_Y = (4, 3, 5, 2, 6, 1, 7)
 ORDER_Y = (0, 1, 2, 3, 7, 6, 5, 4)
 
@@ -21,17 +22,31 @@
     )
 
 
-def chosen(block, wide, to, half):
-    lane = lax.broadcasted_iota(jnp.int32, (192, 128), 1)
-    row = lax.broadcasted_iota(jnp.int32, (192, 128), 0)
+def iotas():
+    return lax.broadcasted_iota(jnp.int32, (192, 128), 1), lax.broadcasted_iota(jnp.int32, (192, 128), 0)
+
+
+def chosen(hit):
+    return jnp.where(hit, 1.0, 0.0).astype(jnp.bfloat16)
+
+
+def wide_choice(block, to, half):
+    lane, row = iotas()
     slot = (lane >= 40).astype(jnp.int32) + (lane >= 80).astype(jnp.int32) + (lane >= 120).astype(jnp.int32)
     inner = lane - 40 * slot
-    odd = to % 2
-    first = jnp.where(wide, odd, 2 - 2 * odd)
-    slots = jnp.where(wide, 3, 2)
-    source = 288 * to - 192 * block + 36 * half + 72 * (slot + first) + inner
-    hit = (source == row) & (inner < 36) & (slot < slots)
-    return jnp.where(hit, 1.0, 0.0).astype(jnp.bfloat16)
+    source = 288 * to - 192 * block + 36 * half + 72 * (slot + lax.rem(to, 2)) + inner
+    return chosen((source == row) & (inner < 36) & (slot < 3))
+
+
+def narrow_choice(block, to, half, side):
+    lane, row = iotas()
+    lane = lane - 64 * side
+    odd = lax.rem(to, 2)
+    cut = 24 + 12 * odd
+    slot = (lane >= cut).astype(jnp.int32)
+    inner = jnp.where(lane >= cut, lane - cut, lane + 12 - 12 * odd)
+    source = 288 * to - 192 * block + 36 * half + 72 * (slot + 2 - 2 * odd) + inner
+    return chosen((source == row) & (lane >= 0) & (lane < 60))
 
 
 def kernel(
@@ -57,7 +72,6 @@
     kind = jnp.where(core == pair % 2, 0, 1)
     giver = jnp.where(kind == 0, (3 * pair + 2 * (y % 2)) // 2, (3 * pair + 1) // 2)
     gives_self = zl == giver
-    sent_kind = jnp.where(split, 1, 0)
     sibling = device(y, x, z, 1 - core)
 
     barrier = pltpu.get_barrier_semaphore()
@@ -65,11 +79,8 @@
     def greet(where):
         pl.semaphore_signal(barrier, inc=1, device_id=where, device_id_type=MESH)
 
-    def providers():
-        for half in (0, 1):
-            at = half * NL + giver
-            for d in range(NY):
-                yield at, device((y + d) % NY, x, at, core)
+    def providers(half):
+        return [device((y + d) % NY, x, half * NL + giver, core) for d in range(NY)]
 
     def signal(sem, where):
         pl.semaphore_signal(sem, inc=1, device_id=where, device_id_type=MESH)
@@ -90,11 +101,12 @@
             greet(device((y + d) % NY, x, z, core))
 
     greet(sibling)
-    for at, where in providers():
-
-        @pl.when(at > z)
-        def _():
-            greet(where)
+    for half in (0, 1):
+
+        @pl.when(half * NL + giver > z)
+        def _():
+            for where in providers(half):
+                greet(where)
 
     for to in range(1, NZ):
 
@@ -122,54 +134,42 @@
         signal(answer_far, device(y, x, z - NL, core))
         across.start()
 
-    for at, where in providers():
-
-        @pl.when(at < z)
-        def _():
-            signal(answer.at[z], where)
-
-    for d in range(1, NY):
-
-        @pl.when(rank((y + d) % NY) < rank(y))
-        def _():
-            signal(answer_y.at[NY - d], device((y + d) % NY, x, z, core))
-
-    for d in range(1, NX):
-
-        @pl.when((x + d) % NX < x)
-        def _():
-            signal(answer_x.at[NX - d], device(y, (x + d) % NX, z, core))
-
     load_a.wait()
     mine = a_own[...]
 
-    def make(k, half):
-        wide = jnp.logical_not(split)
-        tile = jnp.dot(mine, chosen(blk, wide, targets[k], half), preferred_element_type=jnp.float32)
-        tiles[k, half] = tile.astype(jnp.bfloat16)
-
-    make(0, 0)
-    make(0, 1)
+    @pl.when(jnp.logical_not(split))
+    def _():
+        for half in range(2):
+            tile = jnp.dot(mine, wide_choice(blk, targets[0], half), preferred_element_type=jnp.float32)
+            tiles[0, half] = tile.astype(jnp.bfloat16)
 
     @pl.when(split)
     def _():
-        make(1, 0)
-        make(1, 1)
-
-    def tile_copy(k, to):
+        for k in range(2):
+            for half in range(2):
+                low = jnp.dot(mine[0:32], narrow_choice(blk, targets[k], half, 0), preferred_element_type=jnp.float32)
+                high = jnp.dot(mine[32:48], narrow_choice(blk, targets[k], half, 1), preferred_element_type=jnp.float32)
+                tiles[k, half, 0:16] = (low[0:16] + high).astype(jnp.bfloat16)
+                tiles[k, half, 16:32] = low[16:32].astype(jnp.bfloat16)
+
+    def tile_copy(k, to, sort):
         return remote(
-            tiles.at[k, to // NL], a_all.at[sent_kind, slot], tile_send.at[k, to], tile_recv.at[slot],
+            tiles.at[k, to // NL, 0:DEPTH[sort]], a_all.at[sort, slot, 0:DEPTH[sort]], tile_send.at[k, to], tile_recv.at[slot],
             device(targets[k], x, to, core),
         )
 
     def each_tile(to, act):
-        @pl.when((to != z) | (targets[0] != y))
-        def _():
-            act(tile_copy(0, to))
-
-        @pl.when(split & ((to != z) | (targets[1] != y)))
-        def _():
-            act(tile_copy(1, to))
+        outside = [(to != z) | (targets[k] != y) for k in range(2)]
+
+        @pl.when(outside[0] & jnp.logical_not(split))
+        def _():
+            act(tile_copy(0, to, 0))
+
+        for k in range(2):
+
+            @pl.when(outside[k] & split)
+            def _():
+                act(tile_copy(k, to, 1))
 
     def start_tiles(planes, low):
         for to in planes:
@@ -181,6 +181,25 @@
                 each_tile(to, lambda copy: copy.start())
 
     start_tiles(range(NZ - 1), True)
+    for half in (0, 1):
+
+        @pl.when(half * NL + giver < z)
+        def _():
+            for where in providers(half):
+                signal(answer.at[z], where)
+
+    for d in range(1, NY):
+
+        @pl.when(rank((y + d) % NY) < rank(y))
+        def _():
+            signal(answer_y.at[NY - d], device((y + d) % NY, x, z, core))
+
+    for d in range(1, NX):
+
+        @pl.when((x + d) % NX < x)
+        def _():
+            signal(answer_x.at[NX - d], device(y, (x + d) % NX, z, core))
+
     for d in RING_Y:
 
         @pl.when(rank((y + d) % NY) > rank(y))
@@ -217,56 +236,78 @@
 
     @pl.when(gives_self)
     def _():
-        a_all[kind, slot] = tiles[jnp.where(split & (targets[1] == y), 1, 0), zh]
+        @pl.when(split)
+        def _():
+            a_all[1, slot, 0:32] = tiles[jnp.where(targets[1] == y, 1, 0), zh, 0:32]
+
+        @pl.when(jnp.logical_not(split))
+        def _():
+            a_all[0, slot] = tiles[0, zh]
 
     across.wait_recv()
     rest_copies(lambda copy: copy.start())
 
     start_tiles(range(NL, NZ), False)
 
-    def arrival(s):
-        return remote(a_all.at[kind, s], a_all.at[kind, s], tile_send.at[0, 0], tile_recv.at[s], sibling)
-
-    def give(s):
-        return remote(a_all.at[kind, s], a_all.at[kind, s], pair_send.at[s], pair_recv.at[s], sibling)
-
-    def take(s):
-        return remote(a_all.at[1 - kind, s], a_all.at[1 - kind, s], pair_send.at[s], pair_recv.at[s], sibling)
-
-    @pl.when(jnp.logical_not(gives_self))
-    def _():
-        arrival(slot).wait_recv()
-
-    give(slot).start()
-    for d in range(1, NY):
-        s = zh * NY + (y + d) % NY
-        arrival(s).wait_recv()
-        give(s).start()
-    for d in range(NY):
-        s = (1 - zh) * NY + (y + d) % NY
-        arrival(s).wait_recv()
-        give(s).start()
-    for s in range(2 * NY):
-        take(s).wait_recv()
+    def piece(sort, s):
+        return a_all.at[sort, s, 0 : DEPTH[sort]]
+
+    def arrival(sort, s):
+        return remote(piece(sort, s), piece(sort, s), tile_send.at[0, 0], tile_recv.at[s], sibling)
+
+    def give(sort, s):
+        return remote(piece(sort, s), piece(sort, s), pair_send.at[s], pair_recv.at[s], sibling)
+
+    for sort in range(2):
+
+        @pl.when(kind == sort)
+        def _():
+            @pl.when(jnp.logical_not(gives_self))
+            def _():
+                arrival(sort, slot).wait_recv()
+
+            give(sort, slot).start()
+            for half in (zh, 1 - zh):
+                for d in range(NY):
+                    s = half * NY + (y + d) % NY
+                    if d or half is not zh:
+                        arrival(sort, s).wait_recv()
+                        give(sort, s).start()
+            for d in range(NY):
+                give(1 - sort, zh * NY + d).wait_recv()
 
     load_b.wait()
     from_y(zh, own_recv)
 
-    depth = NY * 48
-
-    def product(k, base):
-        left = a_all[k, pl.ds(base, NY)].reshape(depth, 128)
-        right = b_all[pl.ds(base, NY)].reshape(depth, 256)
+    def matmul(sort, base, rows, first, last):
+        left = a_all[sort, pl.ds(base, NY), 0:rows].reshape(NY * rows, 128)
+        right = b_all[pl.ds(base, NY), first:last].reshape(NY * rows, 256)
         return lax.dot_general(left, right, (((0,), (0,)), ((), ())), preferred_element_type=jnp.float32)
+
+    def product(sort, base):
+        if sort == 0:
+            return matmul(0, base, 48, 0, 48)
+        return matmul(1, base, 32, 0, 32)[0:64] + matmul(1, base, 16, 32, 48)[64:128]
 
     base, far_base = zh * NY, (1 - zh) * NY
     wide, narrow = product(0, base), product(1, base)
+    for sort in range(2):
+
+        @pl.when(kind == sort)
+        def _():
+            for d in range(NY):
+                give(1 - sort, (1 - zh) * NY + d).wait_recv()
+
     from_y(1 - zh, rest_recv)
     wide += product(0, far_base)
     narrow += product(1, far_base)
     w = [wide[40 * i : 40 * i + 36] for i in range(3)]
-    n = [narrow[40 * i : 40 * i + 36] for i in range(2)]
     odd = y % 2 == 1
+    none = jnp.zeros((12, 256), jnp.float32)
+    n = [
+        jnp.where(odd, narrow[0:36], jnp.concatenate([none, narrow[0:24]], axis=0)),
+        jnp.where(odd, jnp.concatenate([narrow[36:60], none], axis=0), narrow[24:60]),
+    ]
     sums = (
         jnp.where(odd, n[0], w[0]),
         jnp.where(odd, n[1] + w[0], w[1]),
@@ -301,8 +342,13 @@
     across.wait_send()
     for to in range(NZ):
         each_tile(to, lambda copy: copy.wait_send())
-    for s in range(2 * NY):
-        give(s).wait_send()
+    for sort in range(2):
+
+        @pl.when(kind == sort)
+        def _():
+            for s in range(2 * NY):
+                give(sort, s).wait_send()
+
     own_copies(lambda copy: copy.wait_send())
     rest_copies(lambda copy: copy.wait_send())
     sums_x(lambda copy: copy.wait_send())

time: 35.1 us -> 34.9 us (level)
  the two profiles are of different devices: /device:TPU:224 before, /device:TPU:232 now
where the time goes in v5:
time: 34.9 us; the launch traced here: 34.7 us
  Pallas kernels  34.1 us (98%)
  local copies, waits for them, and re-layouts  0.62 us (2%)
    pallas_call x1, Pallas kernels, body(): pl.pallas_call(kernel, out_shape=pltpu.VMEM((72, 128), jnp.float32), in_s...  34.1 us

profile of v5, /device:TPU:232, one launch (start us, length us, event | category | flops | bytes accessed | tf_op | source)
XLA Modules:
  0.0 34.7 jit_solution(8536795449846688826)
XLA Ops:
  0.0 34.1 %shard_map.28 = f32[72,128]{1,0:T(8,128)S(1)} custom-call(bf16[48,192]{1,0:T(8,128)(2,1)} %bitcast.6, bf16[48,256]{1,0:T(8,128)(2,1)} %bitcast.7), custom_call_target="tpu_custom_call" | custom-call | tf_op jit(solution)/shard_map/pallas_call | solution.py:361
  34.1 0.6 %copy.6 = f32[36,1,256]{2,1,0:T(1,128)} copy(f32[36,1,256]{2,1,0:T(1,128)S(1)} %bitcast.5) | data formatting | bytes 73728

commit v6 on v5

--- a/solution.py
+++ b/solution.py
@@ -63,8 +63,8 @@
 
     load_a = pltpu.make_async_copy(a_ref, a_own, local_sem.at[0])
     load_b = pltpu.make_async_copy(b_ref, b_all.at[slot], local_sem.at[1])
+    load_b.start()
     load_a.start()
-    load_b.start()
 
     split = blk % 3 == 1
     targets = (2 * (blk // 3) + (blk % 3) // 2, 2 * (blk // 3) + 1)
@@ -127,7 +127,8 @@
     partners = rank(y) + x + 1 + per_plane * z + NY * lower + jnp.where(z >= NL, 1, 0)
     pl.semaphore_wait(barrier, partners)
 
-    across = remote(b_ref, b_all.at[slot], far_send.at[0], far_recv.at[0], device(y, x, (z + NL) % NZ, core))
+    load_b.wait()
+    across = remote(b_all.at[slot], b_all.at[slot], far_send.at[0], far_recv.at[0], device(y, x, (z + NL) % NZ, core))
 
     @pl.when(z >= NL)
     def _():
@@ -214,7 +215,7 @@
                 act(remote(src, b_all.at[into], send.at[to], recv.at[y], device(to, x, z, core)))
 
     def own_copies(act):
-        round_y(b_ref, slot, own_send, own_recv, act)
+        round_y(b_all.at[slot], slot, own_send, own_recv, act)
 
     def rest_copies(act):
         round_y(b_all.at[other], other, rest_send, rest_recv, act)
@@ -276,7 +277,6 @@
             for d in range(NY):
                 give(1 - sort, zh * NY + d).wait_recv()
 
-    load_b.wait()
     from_y(zh, own_recv)
 
     def matmul(sort, base, rows, first, last):

time: 34.9 us -> 34.5 us (0.989)
  the two profiles are of different devices: /device:TPU:232 before, /device:TPU:224 now
where the time goes in v6:
time: 34.5 us; the launch traced here: 34.4 us
  Pallas kernels  33.7 us (98%)
  local copies, waits for them, and re-layouts  0.62 us (2%)
    pallas_call x1, Pallas kernels, body(): pl.pallas_call(kernel, out_shape=pltpu.VMEM((72, 128), jnp.float32), in_s...  33.7 us

profile of v6, /device:TPU:224, one launch (start us, length us, event | category | flops | bytes accessed | tf_op | source)
XLA Modules:
  0.0 34.4 jit_solution(9002342695674467037)
XLA Ops:
  0.0 33.7 %shard_map.28 = f32[72,128]{1,0:T(8,128)S(1)} custom-call(bf16[48,192]{1,0:T(8,128)(2,1)} %bitcast.6, bf16[48,256]{1,0:T(8,128)(2,1)} %bitcast.7), custom_call_target="tpu_custom_call" | custom-call | tf_op jit(solution)/shard_map/pallas_call | solution.py:361
  33.7 0.6 %copy.6 = f32[36,1,256]{2,1,0:T(1,128)} copy(f32[36,1,256]{2,1,0:T(1,128)S(1)} %bitcast.5) | data formatting | bytes 73728

commit v7 on v6

--- a/solution.py
+++ b/solution.py
@@ -288,6 +288,12 @@
         if sort == 0:
             return matmul(0, base, 48, 0, 48)
         return matmul(1, base, 32, 0, 32)[0:64] + matmul(1, base, 16, 32, 48)[64:128]
+
+    for d in range(1, NX):
+
+        @pl.when((x + d) % NX > x)
+        def _():
+            pl.semaphore_wait(answer_x.at[d], 1)
 
     base, far_base = zh * NY, (1 - zh) * NY
     wide, narrow = product(0, base), product(1, base)
@@ -317,12 +323,6 @@
     for i, value in enumerate(sums):
         part[i, 0:36] = value[:, 0:128]
         part[i, 36:72] = value[:, 128:256]
-
-    for d in range(1, NX):
-
-        @pl.when((x + d) % NX > x)
-        def _():
-            pl.semaphore_wait(answer_x.at[d], 1)
 
     def sums_x(act):
         for to in range(NX):

time: 34.5 us -> 34.5 us (level)
  no operation moved by 1% of the time
where the time goes in v7:
time: 34.5 us; the launch traced here: 34.3 us
  Pallas kernels  33.7 us (98%)
  local copies, waits for them, and re-layouts  0.62 us (2%)
    pallas_call x1, Pallas kernels, body(): pl.pallas_call(kernel, out_shape=pltpu.VMEM((72, 128), jnp.float32), in_s...  33.7 us

profile of v7, /device:TPU:224, one launch (start us, length us, event | category | flops | bytes accessed | tf_op | source)
XLA Modules:
  0.0 34.3 jit_solution(7132238773970924952)
XLA Ops:
  0.0 33.7 %shard_map.28 = f32[72,128]{1,0:T(8,128)S(1)} custom-call(bf16[48,192]{1,0:T(8,128)(2,1)} %bitcast.6, bf16[48,256]{1,0:T(8,128)(2,1)} %bitcast.7), custom_call_target="tpu_custom_call" | custom-call | tf_op jit(solution)/shard_map/pallas_call | solution.py:361
  33.7 0.6 %copy.6 = f32[36,1,256]{2,1,0:T(1,128)} copy(f32[36,1,256]{2,1,0:T(1,128)S(1)} %bitcast.5) | data formatting | bytes 73728
